TPU v7x, 128 devices: a whole 4x4x4 slice. The times are simulated.
128 devices in a mesh: blk: 8 (over x, z_lo), grp: 16 (over z_hi, y, core).
Axes of the slice: x: 4, y: 4, z: 4 (z_hi: 2, z_lo: 2; z = z_hi * 2 + z_lo), core: 2. Of those that a mesh axis runs over, the one named last changes fastest.
Arguments:
- queries: bfloat16 [65536, 4096], P(('blk', 'grp')), may hold values from -8 to 8
- passages: bfloat16 [16384, 4096], P(('blk', 'grp')), may hold values from -0.75 to 0.75
- positive_ids: int32 [65536], P(('blk', 'grp')), may hold values from 0 to 1023
- hard_ids: int32 [65536, 1], P(('blk', 'grp')), may hold values from 0 to 2047, as said below
Outputs:
- loss: float32 [], replicated
- loss_slope_by_question: bfloat16 [65536, 4096], P(('blk', 'grp'))
- grad_passages: bfloat16 [16384, 4096], P(('blk', 'grp'))
Inputs may be any that keep to these rules, and one draw needn't show every extreme that they name: `hard_ids`: of the 512 entries of one device, at most 64 name passages of any one grp index (rows g * 128 to g * 128 + 127 of the pool); in every batch shard one grp index receives exactly 64 from each device of the shard.
All inputs are finite; a program needn't handle non-finite values.
Results may differ from a plain program's by a relative error of at most 0.017.
Values may be sent and summed in bfloat16 or wider, within the bound.
A program may use at most 192 MiB of HBM per device.

v0:
```python
import functools

import jax
import jax.numpy as jnp
from jax import lax
from jax.experimental import pallas as pl
from jax.experimental.pallas import tpu as pltpu
from jax.sharding import PartitionSpec as P

logit_scaling_coefficient = 20.0
MESH = pl.DeviceIdType.MESH
BF16 = jnp.bfloat16
F32 = jnp.float32
COPIES = 112
NT = (((1,), (1,)), ((), ()))


def rows(start, size, multiple=64):
    return pl.ds(pl.multiple_of(start, multiple), size)


def kernel(
    q_hbm, p_hbm, pos_ref, hid_ref,
    loss_ref, dq_hbm, dp_hbm, other_hbm,
    lbuf, pbuf, qbuf, s, wt, wall, wht, xs, ys, xrf, xrs, yrf, yrs, zrh, zrl, via, mix,
    ids, hs, hin, w2, top, run, hit, lsum, lsend, lrecv, otile, dqt,
    ssem, rsem, csem,
):
    q_dev, width = q_hbm.shape
    p_dev = p_hbm.shape[0]
    half = p_dev // 2
    scale = logit_scaling_coefficient

    b = lax.axis_index("blk")
    g = lax.axis_index("grp")
    x, zl = lax.div(b, 2), lax.rem(b, 2)
    zh, y, core = lax.div(g, 8), lax.div(lax.rem(g, 8), 2), lax.rem(g, 2)
    pb = x * 2 + 1 - zl
    px = [lax.rem(x + k, 4) for k in range(4)]
    py = [lax.rem(y + k, 4) for k in range(4)]
    xp = (px[1] * 2 + zl, g)
    xm = (px[3] * 2 + zl, g)
    yp = (b, zh * 8 + py[1] * 2 + core)
    ym = (b, zh * 8 + py[3] * 2 + core)
    p1 = (pb, g)
    p2 = (pb, lax.rem(g + 8, 16))
    sib = (b, zh * 8 + y * 2 + 1 - core)

    number = {}
    started = {}

    def describe(name, src, dst, peer):
        k = number.setdefault(name, len(number))
        return pltpu.make_async_remote_copy(
            src_ref=src, dst_ref=dst, send_sem=ssem.at[k], recv_sem=rsem.at[k],
            device_id=peer, device_id_type=MESH,
        )

    def send(name, src, dst, peer):
        copy = describe(name, src, dst, peer)
        copy.start()
        started[name] = copy

    def sent(name):
        started.pop(name).wait_send()

    def arrived(name, dst):
        describe(name, dst, dst, sib).wait_recv()

    quarter = half // 2
    moved = half * 3 // 4
    halves = [(0, half), (half, half)]
    by_z = [(0, moved), (p_dev - moved, moved)]
    direct = [(moved, half - moved), (half, half - moved)]
    whole = (0, p_dev)

    def lrow(xx, zz, part=whole):
        return lbuf.at[rows((xx * 2 + zz) * p_dev + part[0], part[1], 16)]

    def prow(yy, zz, part=whole):
        return pbuf.at[rows((yy * 2 + zz) * p_dev + part[0], part[1], 16)]

    def orow(yy, zz):
        return other_hbm.at[rows((yy * 2 + zz) * p_dev, p_dev)]

    local = [
        pltpu.make_async_copy(q_hbm, qbuf.at[pl.ds(0, q_dev)], csem.at[0]),
        pltpu.make_async_copy(p_hbm, lrow(x, zl), csem.at[1]),
        pltpu.make_async_copy(p_hbm, prow(y, zh), csem.at[2]),
    ]
    for copy in local:
        copy.start()
    ids[0] = jnp.broadcast_to(hid_ref[...], ids.shape[1:])
    hs[...] = jnp.zeros(hs.shape, F32)
    top[...] = jnp.full(top.shape, -jnp.inf, F32)
    run[...] = jnp.zeros(run.shape, F32)
    hit[...] = jnp.zeros(hit.shape, F32)

    barrier = pltpu.get_barrier_semaphore()
    for peer in (xp, xm, yp, ym, p1, p2, sib):
        pl.semaphore_signal(barrier, inc=1, device_id=peer, device_id_type=MESH)
    pl.semaphore_wait(barrier, 7)

    own = [p_hbm.at[pl.ds(h * half, half)] for h in range(2)]
    quarters = [(k * quarter, quarter) for k in range(4)]

    for k in range(4):
        send(f"z{k}", p_hbm.at[pl.ds(k * quarter, quarter)], lrow(x, zl, quarters[k]), p1)
    for h in range(2):
        r = 1 - h
        send(f"x+o{h}", own[h], lrow(x, zl, halves[h]), xp)
        send(f"x-o{r}", own[r], lrow(x, zl, halves[r]), xm)
        send(f"y+o{h}", own[h], prow(y, zh, halves[h]), yp)
        send(f"y-o{r}", own[r], prow(y, zh, halves[r]), ym)
    send("ids", ids.at[0], ids.at[1], sib)
    send("q", q_hbm, qbuf.at[pl.ds(q_dev, q_dev)], sib)

    def score_loop(xx, zz):
        c = xx * 2 + zz
        acc = scale * lax.dot_general(
            lbuf[rows(c * p_dev, p_dev), :], qbuf[pl.ds(0, q_dev), :], NT,
            preferred_element_type=F32,
        )
        s[:, rows(c * q_dev, q_dev, q_dev)] = acc
        old = top[0:1]
        peak = jnp.maximum(old, jnp.max(acc, axis=0, keepdims=True))
        total = run[0:1] * jnp.exp(old - peak) + jnp.sum(
            jnp.exp(acc - peak), axis=0, keepdims=True
        )
        row = lax.broadcasted_iota(jnp.int32, acc.shape, 0) + c * p_dev
        top[...] = jnp.broadcast_to(peak, top.shape)
        run[...] = jnp.broadcast_to(total, run.shape)
        hit[...] += jnp.sum(jnp.where(row == pos_ref[...], acc, 0.0), axis=0, keepdims=True)

    def pool_base(yy, zz, cc):
        return (zz * 8 + yy * 2 + cc) * p_dev

    def score_pool(yy, zz):
        slot = yy * 2 + zz
        base = pool_base(yy, zz, core)

        @pl.loop(0, 2)
        def _(k):
            acc = lax.dot_general(
                pbuf[rows(slot * p_dev, p_dev), :], qbuf[rows(k * q_dev, q_dev, q_dev), :], NT,
                preferred_element_type=F32,
            )
            row = lax.broadcasted_iota(jnp.int32, acc.shape, 0) + base
            named = jnp.where(row == ids[k, 0:1, :], scale * acc, 0.0)
            hs[k] += jnp.sum(named, axis=0, keepdims=True)

    oz, oh = 1 - zl, 1 - zh

    for copy in local:
        copy.wait()
    send("oo", prow(y, zh), orow(y, zh), sib)
    score_loop(x, zl)

    def pass_x(name, xx, zz, part, peer):
        send(name, lrow(xx, zz, part), lrow(xx, zz, part), peer)

    def pass_y(name, yy, zz, part, peer):
        send(name, prow(yy, zz, part), prow(yy, zz, part), peer)

    def pass_z(k):
        arrived(f"z{k}", lrow(x, oz, quarters[k]))
        send(f"h{k}", lrow(x, oz, quarters[k]), prow(y, zh, quarters[k]), p2)

    pass_z(0)
    pass_z(1)
    arrived("x+o0", lrow(px[3], zl, halves[0]))
    pass_x("x+f", px[3], zl, halves[0], xp)
    arrived("x-o1", lrow(px[1], zl, halves[1]))
    pass_x("x-f", px[1], zl, halves[1], xm)
    arrived("y+o0", prow(py[3], zh, halves[0]))
    pass_y("y+f", py[3], zh, halves[0], yp)
    arrived("y-o1", prow(py[1], zh, halves[1]))
    pass_y("y-f", py[1], zh, halves[1], ym)
    pass_x("x+p0", x, oz, halves[0], xp)
    arrived("ids", ids.at[1])
    arrived("q", qbuf.at[pl.ds(q_dev, q_dev)])
    score_pool(y, zh)

    pass_z(2)
    arrived("h0", prow(y, oh, quarters[0]))
    arrived("h1", prow(y, oh, quarters[1]))
    pass_y("y+p0", y, oh, halves[0], yp)
    pass_z(3)
    pass_x("x-p1", x, oz, halves[1], xm)
    pass_x("x+p1", x, oz, direct[1], xp)
    pass_x("x-p0", x, oz, direct[0], xm)
    arrived("x+o1", lrow(px[3], zl, halves[1]))
    pass_x("zx1", px[3], zl, by_z[1], p1)
    arrived("x-o0", lrow(px[1], zl, halves[0]))
    pass_x("zx0", px[1], zl, by_z[0], p1)
    arrived("y+o1", prow(py[3], zh, halves[1]))
    send("ty1", prow(py[3], zh, by_z[1]), via.at[1], p2)
    arrived("y-o0", prow(py[1], zh, halves[0]))
    send("ty0", prow(py[1], zh, by_z[0]), via.at[0], p2)
    send("o3", prow(py[3], zh), orow(py[3], zh), sib)
    send("o1", prow(py[1], zh), orow(py[1], zh), sib)
    score_loop(x, oz)
    score_loop(px[3], zl)
    score_loop(px[1], zl)
    arrived("h2", prow(y, oh, quarters[2]))
    arrived("h3", prow(y, oh, quarters[3]))
    pass_y("y-p1", y, oh, halves[1], ym)
    pass_y("y+p1", y, oh, direct[1], yp)
    pass_y("y-p0", y, oh, direct[0], ym)
    send("op", prow(y, oh), orow(y, oh), sib)
    score_pool(py[3], zh)
    score_pool(py[1], zh)
    arrived("x+f", lrow(px[2], zl, halves[0]))
    arrived("x-f", lrow(px[2], zl, halves[1]))
    score_loop(px[2], zl)
    arrived("ty1", via.at[1])
    send("tz1", via.at[1], prow(py[3], oh, by_z[1]), p1)
    score_pool(y, oh)
    arrived("y+f", prow(py[2], zh, halves[0]))
    arrived("y-f", prow(py[2], zh, halves[1]))
    send("o2", prow(py[2], zh), orow(py[2], zh), sib)
    score_pool(py[2], zh)
    arrived("x+p0", lrow(px[3], oz, halves[0]))
    pass_x("x+g", px[3], oz, halves[0], xp)
    arrived("x-p1", lrow(px[1], oz, halves[1]))
    pass_x("x-g", px[1], oz, halves[1], xm)
    arrived("y+p0", prow(py[3], oh, halves[0]))
    pass_y("y+g", py[3], oh, halves[0], yp)
    arrived("y-p1", prow(py[1], oh, halves[1]))
    pass_y("y-g", py[1], oh, halves[1], ym)
    arrived("ty0", via.at[0])
    send("tz0", via.at[0], prow(py[1], oh, by_z[0]), p1)
    arrived("x+p1", lrow(px[3], oz, direct[1]))
    arrived("zx1", lrow(px[3], oz, by_z[1]))
    score_loop(px[3], oz)
    arrived("x-p0", lrow(px[1], oz, direct[0]))
    arrived("zx0", lrow(px[1], oz, by_z[0]))
    score_loop(px[1], oz)
    arrived("y+p1", prow(py[3], oh, direct[1]))
    arrived("tz1", prow(py[3], oh, by_z[1]))
    score_pool(py[3], oh)
    arrived("y-p0", prow(py[1], oh, direct[0]))
    arrived("tz0", prow(py[1], oh, by_z[0]))
    score_pool(py[1], oh)
    arrived("y+g", prow(py[2], oh, halves[0]))
    arrived("y-g", prow(py[2], oh, halves[1]))
    score_pool(py[2], oh)
    send("hs", hs.at[1], hin, sib)
    arrived("x+g", lrow(px[2], oz, halves[0]))
    arrived("x-g", lrow(px[2], oz, halves[1]))
    score_loop(px[2], oz)

    arrived("hs", hin)
    hard = hs[0, 0:1, :] + hin[0:1, :]
    peak = jnp.maximum(top[0:1], hard)
    total = run[0:1] * jnp.exp(top[0:1] - peak) + jnp.exp(hard - peak)
    log_total = peak + jnp.log(total)
    w_hard = jnp.exp(hard - log_total).astype(BF16).astype(F32)
    w2[0] = jnp.broadcast_to(w_hard, w2.shape[1:])
    send("w", w2.at[0], w2.at[1], sib)
    lsum[...] = jnp.broadcast_to(
        jnp.sum(log_total - hit[0:1], axis=1, keepdims=True), lsum.shape
    )
    blocks = s.shape[1] // q_dev

    def weigh(xx, zz):
        c = xx * 2 + zz
        part = s[:, rows(c * q_dev, q_dev, q_dev)]
        row = lax.broadcasted_iota(jnp.int32, part.shape, 0) + c * p_dev
        one = jnp.where(row == pos_ref[...], 1.0, 0.0)
        wt[rows(c * p_dev, p_dev), :] = (jnp.exp(part - log_total) - one).astype(BF16)

    loss_peers = [
        (lax.rem(b + 2 + 4 * lax.rem(x, 2), 8), g),
        (b, zh * 8 + lax.rem(y + 1 + 2 * lax.rem(y, 2), 4) * 2 + core),
        p1,
        p2,
        sib,
        ((3 - x) * 2 + zl, g),
        (b, zh * 8 + (3 - y) * 2 + core),
    ]

    def loss_start(k):
        lsend[k] = lsum[...]
        send(f"l{k}", lsend.at[k], lrecv.at[k], loss_peers[k])

    def loss_finish(k):
        arrived(f"l{k}", lrecv.at[k])
        lsum[...] = lsend[k] + lrecv[k]

    loss_start(0)

    step = 512

    def columns(count):
        return width // 2 if count == p_dev else step

    def loop_part(start, count, store):
        n = columns(count)

        @pl.loop(0, width // n, unroll=min(4, width // n // 2))
        def _(t):
            cols = rows(t * n, n, n)
            store(cols, scale * jnp.dot(
                wt[rows(start, count), :], qbuf[pl.ds(0, q_dev), cols],
                preferred_element_type=F32,
            ))

    def pool_weights(yy, zz, at):
        base = pool_base(yy, zz, core)
        for k in range(2):
            row = lax.broadcasted_iota(jnp.int32, (p_dev, q_dev), 0) + base
            wht[at:at + p_dev, k * q_dev:(k + 1) * q_dev] = jnp.where(
                row == ids[k, 0:1, :], w2[k, 0:1, :], 0.0
            ).astype(BF16)

    def pool_part(count, store):
        n = columns(count)

        @pl.loop(0, width // n, unroll=min(4, width // n // 2))
        def _(t):
            cols = rows(t * n, n, n)
            store(cols, scale * jnp.dot(
                wht[pl.ds(0, count), :], qbuf[:, cols], preferred_element_type=F32
            ))

    z_of = {"x": (oz, zl), "y": (oh, zh)}
    axes = {"x": (xs, xrf, xrs, xp, xm), "y": (ys, yrf, yrs, yp, ym)}

    def piece(a, slot, role, part):
        return axes[a][0].at[slot, rows(z_of[a][role] * p_dev + part[0], part[1], 16)]

    def at(part):
        return pl.ds(part[0], part[1])

    def add_to(dst, *terms):
        @pl.loop(0, width // step, unroll=2)
        def _(t):
            cols = rows(t * step, step, step)
            total = dst[:, cols].astype(F32)
            for term in terms:
                total += term[:, cols].astype(F32)
            dst[:, cols] = total.astype(BF16)

    def send_far(a, role):
        _, rf, _, plus, minus = axes[a]
        send(f"{a}+s2{role}", piece(a, 2, role, halves[0]), rf.at[0, role], plus)
        send(f"{a}-s2{role}", piece(a, 2, role, halves[1]), rf.at[1, role], minus)

    def send_near(a, role):
        _, _, rs, plus, minus = axes[a]
        send(f"{a}+s1{role}", piece(a, 0, role, direct[1]), rs.at[0, role, at(direct[1])], plus)
        send(f"{a}-s1{role}", piece(a, 1, role, direct[0]), rs.at[1, role, at(direct[0])], minus)

    def send_mix_x():
        send("mx1", piece("x", 0, 0, by_z[1]), mix.at[1], p1)
        send("mx0", piece("x", 1, 0, by_z[0]), mix.at[0], p1)

    hop = [xrs.at[1, 0, at(by_z[0])], xrs.at[0, 0, at(by_z[1])]]
    end = [yrs.at[1, 0, at(by_z[0])], yrs.at[0, 0, at(by_z[1])]]

    def send_mix_y():
        send("my1", piece("y", 0, 0, by_z[1]), hop[1], p2)
        send("my0", piece("y", 1, 0, by_z[0]), hop[0], p2)

    def pass_mix_y(h):
        arrived(f"my{h}", hop[h])
        send(f"mz{h}", hop[h], end[h], p1)

    def send_mixed(a, h):
        _, _, rs, plus, minus = axes[a]
        term = mix.at[h] if a == "x" else end[h]
        arrived(f"mx{h}" if a == "x" else f"mz{h}", term)
        mine = piece(a, 1 - h, 1, by_z[h])
        add_to(mine, term)
        send(f"{a}m{h}", mine, rs.at[1 - h, 1, at(by_z[h])], plus if h else minus)

    def send_sum(a, role):
        _, rf, rs, plus, minus = axes[a]
        for d, (sign, peer) in enumerate((("+", plus), ("-", minus))):
            arrived(f"{a}{sign}s2{role}", rf.at[d, role])
            mine = piece(a, d, role, halves[d])
            add_to(mine, rf.at[d, role])
            send(f"{a}{sign}s0{role}", mine, rs.at[d, role, at(halves[d])], peer)

    def sums_arrived(a, role):
        rs = axes[a][2]
        for d, sign in enumerate("+-"):
            arrived(f"{a}{sign}s1{role}", rs.at[d, role, at(direct[1 - d])])
            if role:
                arrived(f"{a}m{1 - d}", rs.at[d, role, at(by_z[1 - d])])
            arrived(f"{a}{sign}s0{role}", rs.at[d, role, at(halves[d])])

    def store_to(ref):
        def store(cols, value):
            ref[:, cols] = value.astype(BF16)
        return store

    place = {1: 0, 3: 1, 2: 2}

    def x_part(k, role):
        zz = z_of["x"][role]
        weigh(px[k], zz)
        loop_part((px[k] * 2 + zz) * p_dev, p_dev, store_to(piece("x", place[k], role, whole)))

    def y_part(k, role):
        pool_weights(py[k], z_of["y"][role], 0)
        pool_part(p_dev, store_to(piece("y", place[k], role, whole)))

    x_part(2, 0)
    send_far("x", 0)
    loss_finish(0)
    loss_start(1)
    arrived("w", w2.at[1])
    y_part(2, 0)
    loss_finish(1)
    send_far("y", 0)
    loss_start(2)
    send("o4", prow(py[3], oh), orow(py[3], oh), sib)
    send("o5", prow(py[1], oh), orow(py[1], oh), sib)
    send("o6", prow(py[2], oh), orow(py[2], oh), sib)
    x_part(1, 0)
    x_part(3, 0)
    send_near("x", 0)
    loss_finish(2)
    loss_start(3)
    send_mix_x()
    y_part(1, 0)
    y_part(3, 0)
    send_near("y", 0)
    loss_finish(3)
    send_mix_y()
    loss_start(4)
    for k in (2, 1, 3):
        x_part(k, 1)
    weigh(x, 0)
    weigh(x, 1)
    send_sum("x", 0)
    y_part(2, 1)
    send_sum("y", 0)
    loss_finish(4)
    loss_start(5)
    send_far("x", 1)
    send_far("y", 1)
    y_part(1, 1)
    y_part(3, 1)
    send_near("x", 1)
    send_near("y", 1)

    for a in "xy":
        sent(f"{a}+s20")
        sent(f"{a}-s20")

    hand_x = xs.at[2, rows(oz * p_dev, p_dev)]
    hand_y = ys.at[2, rows(oh * p_dev, p_dev)]

    def split(first, value):
        low, high = value[:p_dev], value[p_dev:]
        return jnp.where(first, low, high), jnp.where(first, high, low)

    def store_x(cols, value):
        mine, handed = split(zl == 0, value)
        s[:, cols] = mine
        hand_x[:, cols] = handed.astype(BF16)

    def store_y(cols, value):
        mine, handed = split(zh == 0, value)
        s[:, cols] += mine
        hand_y[:, cols] = handed.astype(BF16)

    loop_part(x * 2 * p_dev, 2 * p_dev, store_x)
    pool_weights(y, 0, 0)
    pool_weights(y, 1, p_dev)
    pool_part(2 * p_dev, store_y)
    pass_mix_y(1)
    send_mixed("x", 1)
    send_mixed("x", 0)

    for c in range(blocks):
        wall[:, c * p_dev:(c + 1) * p_dev] = (
            wt[c * p_dev:(c + 1) * p_dev, :].astype(F32).T.astype(BF16)
        )
    loop_rows = blocks * p_dev

    @pl.loop(0, q_dev // 128)
    def _(n):
        part = rows(n * 128, 128, 128)
        names = jnp.broadcast_to(ids[0, 0:1, part].astype(F32), (128, 128)).T
        values = jnp.broadcast_to(w2[0, 0:1, part], (128, 128)).T
        lane = lax.broadcasted_iota(jnp.int32, (128, 128), 1)
        for k in range(2):
            cc = core if k == 0 else 1 - core
            for slot in range(8):
                base = pool_base(slot // 2, slot % 2, cc)
                at = loop_rows + (k * 8 + slot) * p_dev
                wall[part, at:at + p_dev] = jnp.where(
                    names == (lane + base).astype(F32), values, 0.0
                ).astype(BF16)

    arrived("oo", orow(y, zh))
    arrived("o3", orow(py[3], zh))
    arrived("o1", orow(py[1], zh))
    arrived("op", orow(y, oh))
    arrived("o2", orow(py[2], zh))
    arrived("o4", orow(py[3], oh))
    arrived("o5", orow(py[1], oh))
    arrived("o6", orow(py[2], oh))

    tile = dqt.shape[2]
    tiles = width // tile
    pool_rows = pbuf.shape[0]

    def tile_in(t):
        k = lax.rem(t, 2)
        return pltpu.make_async_copy(
            other_hbm.at[:, rows(t * tile, tile, tile)], otile.at[k], csem.at[k]
        )

    def tile_out(t):
        k = lax.rem(t, 2)
        return pltpu.make_async_copy(
            dqt.at[k], dq_hbm.at[:, rows(t * tile, tile, tile)], csem.at[2 + k]
        )

    tile_in(0).start()

    def query_slope(first, last):
        @pl.loop(first, last)
        def _(t):
            k = lax.rem(t, 2)

            @pl.when(t + 1 < tiles)
            def _():
                tile_in(t + 1).start()

            @pl.when(t >= 2)
            def _():
                tile_out(t - 2).wait()

            cols = rows(t * tile, tile, tile)
            tile_in(t).wait()
            acc = jnp.dot(
                wall[:, 0:loop_rows], lbuf[:, cols], preferred_element_type=F32
            )
            acc += jnp.dot(
                wall[:, loop_rows:loop_rows + pool_rows], pbuf[:, cols],
                preferred_element_type=F32,
            )
            acc += jnp.dot(
                wall[:, loop_rows + pool_rows:], otile[k], preferred_element_type=F32
            )
            dqt[k] = (scale * acc).astype(BF16)
            tile_out(t).start()

    query_slope(0, tiles // 4)
    pass_mix_y(0)
    loss_finish(5)
    loss_start(6)
    query_slope(tiles // 4, tiles * 3 // 8)

    parts = [pl.ds(0, moved), pl.ds(moved, p_dev - 2 * moved), pl.ds(p_dev - moved, moved)]
    signs = [(0,), (0, 1), (1,)]
    sums_arrived("y", 0)
    for k, part in enumerate(parts):
        add_to(hand_y.at[part], *(yrs.at[d, 0, part] for d in signs[k]))
        send(f"zh{k}", hand_y.at[part], zrh.at[part], p2)
    send_mixed("y", 1)
    query_slope(tiles * 3 // 8, tiles * 5 // 8)
    sums_arrived("x", 0)
    send_mixed("y", 0)
    send_sum("x", 1)
    send_sum("y", 1)
    for k, part in enumerate(parts):
        arrived(f"zh{k}", zrh.at[part])
        add_to(hand_x.at[part], zrh.at[part], *(xrs.at[d, 0, part] for d in signs[k]))
        send(f"zl{k}", hand_x.at[part], zrl.at[part], p1)
        query_slope(tiles * (10 + 2 * k) // 16, tiles * (12 + 2 * k) // 16)
    loss_finish(6)
    loss_ref[0] = jnp.max(lsum[...]) / (q_dev * lax.axis_size("blk") * lax.axis_size("grp"))

    sums_arrived("x", 1)
    for h, part in enumerate(parts):
        arrived(f"zl{h}", zrl.at[part])

        @pl.loop(0, width // step, unroll=2)
        def _(t):
            cols = rows(t * step, step, step)
            s[part, cols] += (
                xrs[0, 1, part, cols].astype(F32)
                + xrs[1, 1, part, cols].astype(F32)
                + zrl[part, cols].astype(F32)
            )

    sums_arrived("y", 1)
    sent("y+s21")
    sent("y-s21")
    result = ys.at[2, rows(zh * p_dev, p_dev)]
    outs = []
    for h, part in enumerate(parts):
        @pl.loop(0, width // step, unroll=2)
        def _(t):
            cols = rows(t * step, step, step)
            result[part, cols] = (
                s[part, cols]
                + yrs[0, 1, part, cols].astype(F32)
                + yrs[1, 1, part, cols].astype(F32)
            ).astype(BF16)

        copy = pltpu.make_async_copy(result.at[part], dp_hbm.at[part], csem.at[4 + h])
        copy.start()
        outs.append(copy)
    tile_out(tiles - 2).wait()
    tile_out(tiles - 1).wait()
    for copy in outs:
        copy.wait()
    for name in list(started):
        sent(name)


def write(loss_in, slope_in, grad_in, loss_out, slope_out, grad_out, loss, slope, grad, sem):
    pieces = 4
    n = slope.shape[0] // pieces
    moves = [
        (slope_in.at[part], slope.at[part], slope_out.at[part])
        for part in (pl.ds(k * n, n) for k in range(pieces))
    ]
    moves.insert(1, (grad_in, grad, grad_out))
    moves.insert(2, (loss_in, loss, loss_out))
    reads = [
        pltpu.make_async_copy(src, buf, sem.at[0, k]) for k, (src, buf, _) in enumerate(moves)
    ]
    writes = [
        pltpu.make_async_copy(buf, dst, sem.at[1, k]) for k, (_, buf, dst) in enumerate(moves)
    ]
    for copy in reads:
        copy.start()
    for read, copy in zip(reads, writes):
        read.wait()
        copy.start()
    for copy in writes:
        copy.wait()


def shards(queries, passages, positive_ids, hard_ids):
    q_dev, width = queries.shape
    p_dev = passages.shape[0]
    half = p_dev // 2
    moved = half * 3 // 4
    vmem = pltpu.VMEM
    hbm = pl.BlockSpec(memory_space=pl.ANY)
    block = pl.BlockSpec(memory_space=pltpu.VMEM)
    loss, slope, grad, _ = pl.pallas_call(
        kernel,
        out_shape=(
            jax.ShapeDtypeStruct((1,), F32),
            jax.ShapeDtypeStruct((q_dev, width), BF16),
            jax.ShapeDtypeStruct((p_dev, width), BF16),
            jax.ShapeDtypeStruct((8 * p_dev, width), BF16),
        ),
        in_specs=[hbm, hbm, block, block],
        out_specs=(pl.BlockSpec(memory_space=pltpu.SMEM), hbm, hbm, hbm),
        scratch_shapes=[
            vmem((8 * p_dev, width), BF16),
            vmem((8 * p_dev, width), BF16),
            vmem((2 * q_dev, width), BF16),
            vmem((p_dev, 8 * q_dev), F32),
            vmem((8 * p_dev, q_dev), BF16),
            vmem((q_dev, 24 * p_dev), BF16),
            vmem((2 * p_dev, 2 * q_dev), BF16),
            vmem((3, 2 * p_dev, width), BF16),
            vmem((3, 2 * p_dev, width), BF16),
            vmem((2, 2, half, width), BF16),
            vmem((2, 2, p_dev, width), BF16),
            vmem((2, 2, half, width), BF16),
            vmem((2, 2, p_dev, width), BF16),
            vmem((p_dev, width), BF16),
            vmem((p_dev, width), BF16),
            vmem((2, moved, width), BF16),
            vmem((2, moved, width), BF16),
            vmem((2, 8, q_dev), jnp.int32),
            vmem((2, 8, q_dev), F32),
            vmem((8, q_dev), F32),
            vmem((2, 8, q_dev), F32),
            vmem((8, q_dev), F32),
            vmem((8, q_dev), F32),
            vmem((8, q_dev), F32),
            vmem((8, 128), F32),
            vmem((7, 8, 128), F32),
            vmem((7, 8, 128), F32),
            vmem((2, 8 * p_dev, 256), BF16),
            vmem((2, q_dev, 256), BF16),
            pltpu.SemaphoreType.DMA((COPIES,)),
            pltpu.SemaphoreType.DMA((COPIES,)),
            pltpu.SemaphoreType.DMA((7,)),
        ],
        compiler_params=pltpu.CompilerParams(
            collective_id=0, has_side_effects=True, vmem_limit_bytes=63 * 2**20
        ),
        cost_estimate=pl.CostEstimate(
            flops=2 * q_dev * width * 9 * 8 * p_dev,
            bytes_accessed=40 * 2**20,
            transcendentals=2 * 8 * p_dev * q_dev,
        ),
    )(
        queries,
        passages,
        positive_ids.reshape(1, q_dev),
        hard_ids.reshape(1, q_dev),
    )
    loss, slope, grad = pl.pallas_call(
        write,
        out_shape=(
            jax.ShapeDtypeStruct((1,), F32),
            jax.ShapeDtypeStruct(slope.shape, BF16),
            jax.ShapeDtypeStruct(grad.shape, BF16),
        ),
        in_specs=[hbm, hbm, hbm],
        out_specs=(hbm, hbm, hbm),
        scratch_shapes=[
            pltpu.SMEM((1,), F32),
            vmem(slope.shape, BF16),
            vmem(grad.shape, BF16),
            pltpu.SemaphoreType.DMA((2, 6)),
        ],
        compiler_params=pltpu.CompilerParams(vmem_limit_bytes=63 * 2**20),
    )(loss, slope, grad)
    return loss[0], slope, grad


def solution(mesh):
    return jax.shard_map(
        shards,
        mesh=mesh,
        in_specs=(
            P(("blk", "grp"), None),
            P(("blk", "grp"), None),
            P(("blk", "grp")),
            P(("blk", "grp"), None),
        ),
        out_specs=(P(), P(("blk", "grp"), None), P(("blk", "grp"), None)),
        check_vma=False,
    )
```

profile of v0, /device:TPU:0, one launch (start us, length us, event | category | flops | bytes accessed | tf_op | source)
XLA Modules:
  0.0 149.3 jit_solution(3276532599545895650)
XLA Ops:
  0.6 143.6 %shard_map.67 = (f32[1]{0:T(128)}, bf16[512,4096]{1,0:T(8,128)(2,1)}, bf16[128,4096]{1,0:T(8,128)(2,1)}, bf16[1024,4096]{1,0:T(8,128)(2,1)}) custom-call(bf16[512,4096]{1,0:T(8,128)(2,1)} %q_hbm.1, bf16[128,4096]{1,0:T(8,128)(2,1)} %p_hbm.1, s32[1,512]{1,0:T(1,128)} %bitcast.3, s32[1,512]{1,0:T(1,128)} %bitcast.4), custom_call_target="tpu_custom_call" | custom-call | flops 38654705664 | bytes 41943040 | tf_op jit(solution)/shard_map/pallas_call | solution.py:652
  144.2 5.0 %shard_map.68 = (f32[1]{0:T(128)}, bf16[512,4096]{1,0:T(8,128)(2,1)}, bf16[128,4096]{1,0:T(8,128)(2,1)}) custom-call(f32[1]{0:T(128)} %get-tuple-element.9.loss_in, bf16[512,4096]{1,0:T(8,128)(2,1)} %get-tuple-element.10.slope_in, bf16[128,4096]{1,0:T(8,128)(2,1)} %get-tuple-element.11.grad_in), custom_call_target="tpu_custom_call" | custom-call | tf_op jit(solution)/shard_map/pallas_call | solution.py:710
where the time goes:
time: 150 us; the launch traced here: 149 us
  Pallas kernels  149 us (99%)
    pallas_call x1, Pallas kernels, shards(): pl.pallas_call(kernel, out_shape=(jax.ShapeDtypeStruct((1,), F32), jax.Sh...  144 us
    pallas_call x1, Pallas kernels, shards(): pl.pallas_call(write, out_shape=(jax.ShapeDtypeStruct((1,), F32), jax.Sha...  4.95 us

commit v1 on v0

--- a/solution.py
+++ b/solution.py
@@ -12,7 +12,6 @@
 BF16 = jnp.bfloat16
 F32 = jnp.float32
 COPIES = 112
-NT = (((1,), (1,)), ((), ()))
 
 
 def rows(start, size, multiple=64):
@@ -22,7 +21,7 @@
 def kernel(
     q_hbm, p_hbm, pos_ref, hid_ref,
     loss_ref, dq_hbm, dp_hbm, other_hbm,
-    lbuf, pbuf, qbuf, s, wt, wall, wht, xs, ys, xrf, xrs, yrf, yrs, zrh, zrl, via, mix,
+    lbuf, pbuf, qbuf, s, wt, wall, wht, stage, xrf, xrs, yrf, yrs, zrh, zrl, via, mix,
     ids, hs, hin, w2, top, run, hit, lsum, lsend, lrecv, otile, dqt,
     ssem, rsem, csem,
 ):
@@ -30,6 +29,9 @@
     p_dev = p_hbm.shape[0]
     half = p_dev // 2
     scale = logit_scaling_coefficient
+    slots = 6 * p_dev
+    xs = stage.at[pl.ds(0, slots)]
+    ys = stage.at[pl.ds(slots, slots)]
 
     b = lax.axis_index("blk")
     g = lax.axis_index("grp")
@@ -115,12 +117,25 @@
     send("ids", ids.at[0], ids.at[1], sib)
     send("q", q_hbm, qbuf.at[pl.ds(q_dev, q_dev)], sib)
 
+    def turn(k):
+        @pl.loop(0, width // q_dev)
+        def _(t):
+            cols = rows(t * q_dev, q_dev, q_dev)
+            stage[pl.ds(k * slots, q_dev), cols] = qbuf[pl.ds(k * q_dev, q_dev), cols].T
+
+    def score(table, start, k):
+        total = jnp.zeros((p_dev, q_dev), F32)
+        for t in range(width // q_dev):
+            cols = pl.ds(t * q_dev, q_dev)
+            total += jnp.dot(
+                table[rows(start, p_dev), cols], stage[rows(k * slots, q_dev, 256), cols],
+                preferred_element_type=F32,
+            )
+        return scale * total
+
     def score_loop(xx, zz):
         c = xx * 2 + zz
-        acc = scale * lax.dot_general(
-            lbuf[rows(c * p_dev, p_dev), :], qbuf[pl.ds(0, q_dev), :], NT,
-            preferred_element_type=F32,
-        )
+        acc = score(lbuf, c * p_dev, 0)
         s[:, rows(c * q_dev, q_dev, q_dev)] = acc
         old = top[0:1]
         peak = jnp.maximum(old, jnp.max(acc, axis=0, keepdims=True))
@@ -141,12 +156,9 @@
 
         @pl.loop(0, 2)
         def _(k):
-            acc = lax.dot_general(
-                pbuf[rows(slot * p_dev, p_dev), :], qbuf[rows(k * q_dev, q_dev, q_dev), :], NT,
-                preferred_element_type=F32,
-            )
+            acc = score(pbuf, slot * p_dev, k)
             row = lax.broadcasted_iota(jnp.int32, acc.shape, 0) + base
-            named = jnp.where(row == ids[k, 0:1, :], scale * acc, 0.0)
+            named = jnp.where(row == ids[k, 0:1, :], acc, 0.0)
             hs[k] += jnp.sum(named, axis=0, keepdims=True)
 
     oz, oh = 1 - zl, 1 - zh
@@ -154,7 +166,7 @@
     for copy in local:
         copy.wait()
     send("oo", prow(y, zh), orow(y, zh), sib)
-    score_loop(x, zl)
+    turn(0)
 
     def pass_x(name, xx, zz, part, peer):
         send(name, lrow(xx, zz, part), lrow(xx, zz, part), peer)
@@ -179,7 +191,7 @@
     pass_x("x+p0", x, oz, halves[0], xp)
     arrived("ids", ids.at[1])
     arrived("q", qbuf.at[pl.ds(q_dev, q_dev)])
-    score_pool(y, zh)
+    turn(1)
 
     pass_z(2)
     arrived("h0", prow(y, oh, quarters[0]))
@@ -199,6 +211,7 @@
     send("ty0", prow(py[1], zh, by_z[0]), via.at[0], p2)
     send("o3", prow(py[3], zh), orow(py[3], zh), sib)
     send("o1", prow(py[1], zh), orow(py[1], zh), sib)
+    score_loop(x, zl)
     score_loop(x, oz)
     score_loop(px[3], zl)
     score_loop(px[1], zl)
@@ -208,6 +221,7 @@
     pass_y("y+p1", y, oh, direct[1], yp)
     pass_y("y-p0", y, oh, direct[0], ym)
     send("op", prow(y, oh), orow(y, oh), sib)
+    score_pool(y, zh)
     score_pool(py[3], zh)
     score_pool(py[1], zh)
     arrived("x+f", lrow(px[2], zl, halves[0]))
@@ -328,7 +342,8 @@
     axes = {"x": (xs, xrf, xrs, xp, xm), "y": (ys, yrf, yrs, yp, ym)}
 
     def piece(a, slot, role, part):
-        return axes[a][0].at[slot, rows(z_of[a][role] * p_dev + part[0], part[1], 16)]
+        start = (slot * 2 + z_of[a][role]) * p_dev + part[0]
+        return axes[a][0].at[rows(start, part[1], 16)]
 
     def at(part):
         return pl.ds(part[0], part[1])
@@ -451,8 +466,8 @@
         sent(f"{a}+s20")
         sent(f"{a}-s20")
 
-    hand_x = xs.at[2, rows(oz * p_dev, p_dev)]
-    hand_y = ys.at[2, rows(oh * p_dev, p_dev)]
+    hand_x = xs.at[rows((4 + oz) * p_dev, p_dev)]
+    hand_y = ys.at[rows((4 + oh) * p_dev, p_dev)]
 
     def split(first, value):
         low, high = value[:p_dev], value[p_dev:]
@@ -594,7 +609,7 @@
     sums_arrived("y", 1)
     sent("y+s21")
     sent("y-s21")
-    result = ys.at[2, rows(zh * p_dev, p_dev)]
+    result = ys.at[rows((4 + zh) * p_dev, p_dev)]
     outs = []
     for h, part in enumerate(parts):
         @pl.loop(0, width // step, unroll=2)
@@ -625,7 +640,7 @@
         for part in (pl.ds(k * n, n) for k in range(pieces))
     ]
     moves.insert(1, (grad_in, grad, grad_out))
-    moves.insert(2, (loss_in, loss, loss_out))
+    moves.append((loss_in, loss, loss_out))
     reads = [
         pltpu.make_async_copy(src, buf, sem.at[0, k]) for k, (src, buf, _) in enumerate(moves)
     ]
@@ -667,8 +682,7 @@
             vmem((8 * p_dev, q_dev), BF16),
             vmem((q_dev, 24 * p_dev), BF16),
             vmem((2 * p_dev, 2 * q_dev), BF16),
-            vmem((3, 2 * p_dev, width), BF16),
-            vmem((3, 2 * p_dev, width), BF16),
+            vmem((12 * p_dev, width), BF16),
             vmem((2, 2, half, width), BF16),
             vmem((2, 2, p_dev, width), BF16),
             vmem((2, 2, half, width), BF16),

time: 150 us -> 148 us (0.987)
  Pallas kernels: 149 us -> 147 us
    pallas_call x1, Pallas kernels: 144 us -> 142 us  [shards(): pl.pallas_call(kernel, out_shape=(jax.ShapeDtypeStruct((1,), F32), jax.Sh...]
where the time goes in v1:
time: 148 us
  Pallas kernels  147 us (99%)
    pallas_call x1, Pallas kernels, shards(): pl.pallas_call(kernel, out_shape=(jax.ShapeDtypeStruct((1,), F32), jax.Sh...  142 us
    pallas_call x1, Pallas kernels, shards(): pl.pallas_call(write, out_shape=(jax.ShapeDtypeStruct((1,), F32), jax.Sha...  4.96 us

profile of v1, /device:TPU:0, one launch (start us, length us, event | category | flops | bytes accessed | tf_op | source)
XLA Modules:
  0.0 147.8 jit_solution(3032465678852818427)
XLA Ops:
  0.6 142.0 %shard_map.67 = (f32[1]{0:T(128)}, bf16[512,4096]{1,0:T(8,128)(2,1)}, bf16[128,4096]{1,0:T(8,128)(2,1)}, bf16[1024,4096]{1,0:T(8,128)(2,1)}) custom-call(bf16[512,4096]{1,0:T(8,128)(2,1)} %q_hbm.1, bf16[128,4096]{1,0:T(8,128)(2,1)} %p_hbm.1, s32[1,512]{1,0:T(1,128)} %bitcast.3, s32[1,512]{1,0:T(1,128)} %bitcast.4), custom_call_target="tpu_custom_call" | custom-call | flops 38654705664 | bytes 41943040 | tf_op jit(solution)/shard_map/pallas_call | solution.py:667
  142.6 5.0 %shard_map.68 = (f32[1]{0:T(128)}, bf16[512,4096]{1,0:T(8,128)(2,1)}, bf16[128,4096]{1,0:T(8,128)(2,1)}) custom-call(f32[1]{0:T(128)} %get-tuple-element.9.loss_in, bf16[512,4096]{1,0:T(8,128)(2,1)} %get-tuple-element.10.slope_in, bf16[128,4096]{1,0:T(8,128)(2,1)} %get-tuple-element.11.grad_in), custom_call_target="tpu_custom_call" | custom-call | tf_op jit(solution)/shard_map/pallas_call | solution.py:724

commit v2 on v1

--- a/solution.py
+++ b/solution.py
@@ -639,8 +639,8 @@
         (slope_in.at[part], slope.at[part], slope_out.at[part])
         for part in (pl.ds(k * n, n) for k in range(pieces))
     ]
-    moves.insert(1, (grad_in, grad, grad_out))
-    moves.append((loss_in, loss, loss_out))
+    moves.insert(0, (grad_in, grad, grad_out))
+    moves.insert(0, (loss_in, loss, loss_out))
     reads = [
         pltpu.make_async_copy(src, buf, sem.at[0, k]) for k, (src, buf, _) in enumerate(moves)
     ]
@@ -649,9 +649,9 @@
     ]
     for copy in reads:
         copy.start()
-    for read, copy in zip(reads, writes):
-        read.wait()
-        copy.start()
+    for k in (1, 2, 0, *range(3, len(moves))):
+        reads[k].wait()
+        writes[k].start()
     for copy in writes:
         copy.wait()
 

time: 148 us -> 148 us (level)
  no operation moved by 1% of the time
where the time goes in v2:
time: 148 us
  Pallas kernels  147 us (99%)
    pallas_call x1, Pallas kernels, shards(): pl.pallas_call(kernel, out_shape=(jax.ShapeDtypeStruct((1,), F32), jax.Sh...  142 us
    pallas_call x1, Pallas kernels, shards(): pl.pallas_call(write, out_shape=(jax.ShapeDtypeStruct((1,), F32), jax.Sha...  4.95 us

profile of v2, /device:TPU:0, one launch (start us, length us, event | category | flops | bytes accessed | tf_op | source)
XLA Modules:
  0.0 147.8 jit_solution(8708683975376813001)
XLA Ops:
  0.6 142.0 %shard_map.67 = (f32[1]{0:T(128)}, bf16[512,4096]{1,0:T(8,128)(2,1)}, bf16[128,4096]{1,0:T(8,128)(2,1)}, bf16[1024,4096]{1,0:T(8,128)(2,1)}) custom-call(bf16[512,4096]{1,0:T(8,128)(2,1)} %q_hbm.1, bf16[128,4096]{1,0:T(8,128)(2,1)} %p_hbm.1, s32[1,512]{1,0:T(1,128)} %bitcast.3, s32[1,512]{1,0:T(1,128)} %bitcast.4), custom_call_target="tpu_custom_call" | custom-call | flops 38654705664 | bytes 41943040 | tf_op jit(solution)/shard_map/pallas_call | solution.py:667
  142.6 5.0 %shard_map.68 = (f32[1]{0:T(128)}, bf16[512,4096]{1,0:T(8,128)(2,1)}, bf16[128,4096]{1,0:T(8,128)(2,1)}) custom-call(f32[1]{0:T(128)} %get-tuple-element.9.loss_in, bf16[512,4096]{1,0:T(8,128)(2,1)} %get-tuple-element.10.slope_in, bf16[128,4096]{1,0:T(8,128)(2,1)} %get-tuple-element.11.grad_in), custom_call_target="tpu_custom_call" | custom-call | tf_op jit(solution)/shard_map/pallas_call | solution.py:724
